TPU v7x, 768 devices: a whole 4x8x12 slice. The times are simulated.
768 devices in a mesh: outer: 16 (over z_hi, x, core), inner: 48 (over y, z_lo).
Axes of the slice: x: 4, y: 8, z: 12 (z_hi: 2, z_lo: 6; z = z_hi * 6 + z_lo), core: 2. Of those that a mesh axis runs over, the one named last changes fastest.
Arguments:
- acts: bfloat16 [4096, 12288], P('outer', 'inner'), may hold values from -6 to 6
- codes: bfloat16 [12288, 6144], P('inner', 'outer'), may hold values from -1.6953125 to 1.6953125
- scales: float32 [48, 12288], P('outer', 'inner'), may hold values from 0.0027063293 to 0.027063293
- routes: int32 [4096, 2], P('outer'), may hold values from 0 to 7, as said below
- route_logits: float32 [4096, 2], P('outer'), may hold values from -6 to 6
- cotangent: bfloat16 [4096, 6144], P('outer'), may hold values from -6 to 6
Outputs:
- mixed: bfloat16 [4096, 6144], P('outer', 'inner')
- act_grad: bfloat16 [4096, 12288], P('outer', 'inner')
- weight_grad: float32 [12288, 6144], P('inner', 'outer')
Inputs may be any that keep to these rules, and one draw needn't show every extreme that they name: `routes`: each token names expert 0 exactly once and one other expert.
All inputs are finite; a program needn't handle non-finite values.
Results may differ from a plain program's by a relative error of at most 0.015.
Values may be sent and summed in bfloat16 or wider, within the bound.
A program may use at most 64 MiB of HBM per device.

v0:
```python
import jax
import jax.numpy as jnp
from jax import lax
from jax.sharding import PartitionSpec as P

BLOCK = 128


def dequantize(stored, factors):
    expanded = jnp.repeat(factors.T, BLOCK, axis=1)
    return (stored.astype(jnp.float32) * expanded).astype(jnp.bfloat16)


def local(acts, codes, scales, routes, route_logits, cotangent):
    full_codes, full_scales = (
        lax.all_gather(codes, "outer", axis=1, tiled=True),
        lax.all_gather(scales.astype(jnp.bfloat16), "outer", axis=0, tiled=True).astype(
            scales.dtype
        ),
    )
    weight = dequantize(full_codes, full_scales)
    probs = jax.nn.softmax(route_logits, axis=-1)
    coef = jnp.sum(probs * (routes == 0).astype(jnp.float32), axis=-1)
    partial_value = coef[:, None] * jnp.dot(acts, weight, preferred_element_type=jnp.float32)
    mixed = lax.psum_scatter(partial_value, "inner", scatter_dimension=1, tiled=True).astype(
        jnp.bfloat16
    )
    scaled = (coef[:, None] * cotangent.astype(jnp.float32)).astype(jnp.bfloat16)
    act_grad = lax.dot_general(
        scaled, weight, (((1,), (1,)), ((), ())), preferred_element_type=jnp.float32
    ).astype(jnp.bfloat16)
    term = jnp.dot(acts.T, scaled, preferred_element_type=jnp.float32).astype(jnp.bfloat16)
    term = lax.optimization_barrier(term)
    weight_grad = lax.psum_scatter(
        term.astype(jnp.float32).astype(jnp.bfloat16), "outer", scatter_dimension=1, tiled=True
    ).astype(jnp.float32)
    return (mixed, act_grad, weight_grad)


def solution(mesh):
    in_specs = (
        P("outer", "inner"),
        P("inner", "outer"),
        P("outer", "inner"),
        P("outer", None),
        P("outer", None),
        P("outer", None),
    )
    out_specs = (P("outer", "inner"), P("outer", "inner"), P("inner", "outer"))
    return jax.shard_map(local, mesh=mesh, in_specs=in_specs, out_specs=out_specs, check_vma=False)
```

profile of v0, /device:TPU:6, one launch (start us, length us, event | category | flops | bytes accessed | tf_op | source)
XLA Modules:
  0.0 573.9 jit_solution(15761079433174745530)
XLA Ops:
  7.2 0.0 copy-start
  7.2 0.0 all-gather.3.cloned.1.call-start
  7.2 0.7 all-gather.3.cloned.1.call-update
  7.9 0.0 reduce-scatter.5.cloned.1.call-start
  8.0 0.7 reduce_max.9
  8.7 0.7 fusion.6
  9.4 0.7 fusion.5
  10.1 0.0 copy-done
  10.1 0.0 copy-start.3
  10.1 4.9 fusion.1
  15.1 0.0 reduce-scatter.5.cloned.1.call-update
  15.1 0.0 reduce-scatter.3.cloned.1.call-start
  15.1 0.0 copy-done.3
  15.1 33.3 %all-gather = bf16[16,3,256]{2,1,0:T(4,128)(2,1)S(1)} all-gather(bf16[1,3,256]{2,1,0:T(4,128)(2,1)S(1)} %convert_bitcast_fusion), channel_id=1, replica_groups=mesh['outer'=16,'inner'=48] {'outer'}, dimensions={0}, use_global_device_ids=true | all-gather | bytes 26112 | tf_op jit(solution)/shard_map/all_gather | solution.py:17
  48.5 0.1 copy.15
  48.6 63.4 %all-gather.3.cloned.1.call-done = bf16[256,6144]{1,0:T(8,128)(2,1)} async-done(((bf16[256,384]{1,0:T(8,128)(2,1)}), bf16[256,6144]{1,0:T(8,128)(2,1)}) %all-gather.3.cloned.1.call-update) | async-done | bytes 3145744 | tf_op jit(solution)/shard_map/all_gather | solution.py:16
  112.0 0.0 copy-start.2
  112.0 1.8 broadcast_in_dim.2
  113.8 0.0 copy-start.1
  113.8 2.7 copy-done.1
  116.5 0.0 copy-done.2
  116.5 5.7 fusion
  122.2 0.0 reduce-scatter.3.cloned.1.call-update
  122.2 114.7 %reduce-scatter.5.cloned.1.call-done = bf16[256,384]{0,1:T(8,128)(2,1)} async-done(((bf16[256,6144]{0,1:T(8,128)(2,1)}), bf16[256,384]{0,1:T(8,128)(2,1)}) %reduce-scatter.5.cloned.1.call-update) | async-done | bytes 196624 | tf_op jit(solution)/shard_map/reduce_scatter | solution.py:34
  236.9 1.8 copy.17
  238.7 6.6 %fusion.4 = bf16[256,256]{1,0:T(8,128)(2,1)} fusion(bf16[256,6144]{1,0:T(8,128)(2,1)} %param.11, f32[256]{0:T(256)S(1)} %fusion.5, f32[32,8,48,128]{3,2,1,0:T(8,128)} %bitcast.17, bf16[256,6144]{1,0:T(8,128)(2,1)S(1)} %copy-done.2), kind=kOutput, calls=%fused_computation.8 | convolution fusion | flops 814809088 | bytes 12715008 | tf_op jit(solution)/shard_map/dot_general | solution.py:29
  245.4 320.4 %reduce-scatter.3.cloned.1.call-done = f32[256,128]{0,1:T(8,128)} async-done(((f32[256,6144]{0,1:T(8,128)}), f32[256,128]{0,1:T(8,128)}) %reduce-scatter.3.cloned.1.call-update) | async-done | bytes 131088 | tf_op jit(solution)/shard_map/reduce_scatter | solution.py:25
  565.8 0.9 convert_element_type.37
  566.7 0.7 copy.16
  (2 shorter events, 0.0 us)
Async XLA Ops:
  7.2 2.9 copy-start
  7.2 104.9 %all-gather.3.cloned.1.call-start = ((), (), s32[]{:S(2)}) async-start(), calls=%async_computation.2 | async-start | bytes 3342336 | tf_op jit(solution)/shard_map/all_gather | solution.py:16
  7.9 229.0 %reduce-scatter.5.cloned.1.call-start = ((), (), s32[]{:S(2)}) async-start(), calls=%async_computation.4 | async-start | bytes 3342336 | tf_op jit(solution)/shard_map/reduce_scatter | solution.py:34
  10.1 5.0 copy-start.3
  15.1 550.7 %reduce-scatter.3.cloned.1.call-start = ((), (), s32[]{:S(2)}) async-start(), calls=%async_computation.3 | async-start | bytes 6422528 | tf_op jit(solution)/shard_map/reduce_scatter | solution.py:25
  112.0 4.4 copy-start.2
  113.8 2.7 copy-start.1
Sparse Core Ops, SparseCore 0:
  11.7 100.2 all-gather.2
  117.5 119.3 reduce-scatter.4
  240.1 325.6 reduce-scatter.2
where the time goes:
time: 574 us
  waiting for transfers between devices  499 us (87%)
  blocking collectives  33.3 us (6%)
  matrix products  17.3 us (3%)
  between operations  13.8 us (2%)
  local copies, waits for them, and re-layouts  7.09 us (1%)
    reduce_scatter x1, waiting for transfers between devices, local(): lax.psum_scatter(partial_value, 'inner', scatter_dimension=1, tiled=True)  320 us
    reduce_scatter x1, waiting for transfers between devices, local(): lax.psum_scatter(term.astype(jnp.float32).astype(jnp.bfloat16), 'outer',...  115 us
    all_gather x1, waiting for transfers between devices, local(): lax.all_gather(codes, 'outer', axis=1, tiled=True)  63.4 us
    all_gather x1, blocking collectives, local(): lax.all_gather(scales.astype(jnp.bfloat16), 'outer', axis=0, tiled=True)  33.3 us
  transfers between devices with their start and end apart: 3, of which 3 were waited for; matrix products, arithmetic and copies ran while one was open for 4% of the time, Pallas kernels for 0%

commit v1 on v0

v1 whole, which is shorter than its diff:
```python
import jax
import jax.numpy as jnp
from jax import lax
from jax.experimental import pallas as pl
from jax.experimental.pallas import tpu as pltpu
from jax.sharding import PartitionSpec as P

MESH = pl.DeviceIdType.MESH
BF16 = jnp.bfloat16
F32 = jnp.float32
NX, NY, NZ, NO = 4, 8, 6, 16
TOK, FFD, COLS = 256, 256, 384
HALF = FFD // 2
N_A, N_B, N_C = 24, 6, 14


def kernel(
    acts_ref, codes_ref, scales_ref, routes_ref, logits_ref, cot_ref,
    mixed_ref, act_grad_ref, wgrad_ref,
    weight, scaled, coef, acts_t, term_out, term_in, term,
    x1_out, x1_in, x2_out, x2_in, z_out, z_in,
    y_out, y_in, m_own, m_out, m_in, acc,
    a_send, a_recv, b_send, b_recv, c_send, c_recv, m_send, m_recv,
):
    o = lax.axis_index("outer")
    i = lax.axis_index("inner")
    core = lax.rem(o, 2)
    x = lax.rem(lax.div(o, 2), NX)
    hi = lax.div(o, 2 * NX)
    y = lax.div(i, NZ)
    z = lax.rem(i, NZ)

    def out_index(hi_, x_, core_):
        return (hi_ * NX + x_) * 2 + core_

    def xp(n):
        return lax.rem(x + n + NX, NX)

    def yp(n):
        return lax.rem(y + n + NY, NY)

    sibling = (out_index(hi, x, 1 - core), i)
    partner = (out_index(1 - hi, x, core), i)
    right, left = (out_index(hi, xp(1), core), i), (out_index(hi, xp(-1), core), i)
    up, down = (o, yp(1) * NZ + z), (o, yp(-1) * NZ + z)

    barrier = pltpu.get_barrier_semaphore()
    for peer in (sibling, partner, right, left, up, down):
        pl.semaphore_signal(barrier, inc=1, device_id=peer, device_id_type=MESH)
    for n in range(1, NZ):
        pl.semaphore_signal(barrier, inc=1, device_id=(o, y * NZ + lax.rem(z + n, NZ)), device_id_type=MESH)

    for b in range(3):
        cols = pl.ds(b * 128, 128)
        weight[o, :, cols] = (codes_ref[:, cols].astype(F32) * scales_ref[:, b : b + 1]).astype(BF16)
    pl.semaphore_wait(barrier, 6 + NZ - 1)

    sent = []

    def send(src, dst, ssem, rsem, peer):
        copy = pltpu.make_async_remote_copy(
            src_ref=src, dst_ref=dst, send_sem=ssem, recv_sem=rsem, device_id=peer, device_id_type=MESH
        )
        copy.start()
        sent.append(copy)
        return copy

    def block(slot, half):
        return weight.at[slot, pl.ds(half * HALF, HALF)]

    def send_a(n, slot, half, peer):
        ref = block(slot, half)
        return send(ref, ref, a_send.at[n], a_recv.at[n], peer)

    a_z = [send_a(h, o, h, partner) for h in range(2)]
    a_r = [[send_a(2 + h, o, h, right) for h in range(2)], None]
    a_l = [[send_a(4 + h, o, h, left) for h in range(2)], None]

    def share(n, slot):
        ref = weight.at[slot]
        return send(ref, ref, a_send.at[16 + n], a_recv.at[16 + n], sibling)

    a_s = [share(0, o)]

    lg = logits_ref[...]
    top = jnp.max(lg, axis=-1, keepdims=True)
    ex = jnp.exp(lg - top)
    probs = ex / jnp.sum(ex, axis=-1, keepdims=True)
    coef[...] = jnp.sum(probs * (routes_ref[...] == 0).astype(F32), axis=-1, keepdims=True)
    acts_t[...] = acts_ref[...].T

    def scale_block(n, carry):
        cols = pl.ds(pl.multiple_of(n * COLS, 128), COLS)
        scaled[n] = (coef[...] * cot_ref[:, cols].astype(F32)).astype(BF16)
        return carry

    lax.fori_loop(0, NO, scale_block, 0)

    def term_other(n, carry):
        term_out[n] = jnp.dot(acts_t[...], scaled[2 * n + 1 - core], preferred_element_type=F32).astype(BF16)
        return carry

    lax.fori_loop(0, 8, term_other, 0)
    b_pair = send(term_out, term_in, b_send.at[0], b_recv.at[0], sibling)

    def forward(stage, hi_):
        base = (6, 14)[stage]
        got_r, got_l = a_r[stage], a_l[stage]
        got_r[0].wait_recv()
        f_r = send_a(base, out_index(hi_, xp(-1), core), 0, right)
        got_l[1].wait_recv()
        f_l = send_a(base + 1, out_index(hi_, xp(1), core), 1, left)
        got_r[1].wait_recv()
        a_s.append(share(1 + 4 * stage, out_index(hi_, xp(-1), core)))
        got_l[0].wait_recv()
        a_s.append(share(2 + 4 * stage, out_index(hi_, xp(1), core)))
        return f_r, f_l

    def finish(stage, hi_, f_r, f_l):
        f_r.wait_recv()
        f_l.wait_recv()
        a_s.append(share(3 + 4 * stage, out_index(hi_, xp(2), core)))

    f_own = forward(0, hi)

    def term_own(n, carry):
        term[n] = jnp.dot(acts_t[...], scaled[2 * n + core], preferred_element_type=F32).astype(BF16)
        return carry

    lax.fori_loop(0, 8, term_own, 0)

    finish(0, hi, *f_own)
    p_slot = out_index(1 - hi, x, core)
    a_r[1], a_l[1] = [], []
    for h in range(2):
        a_z[h].wait_recv()
        a_r[1].append(send_a(8 + h, p_slot, h, right))
        a_l[1].append(send_a(12 + h, p_slot, h, left))
    a_s.append(share(4, p_slot))
    f_far = forward(1, 1 - hi)

    b_pair.wait_recv()

    def far_half(w, half):
        rows = pl.ds(half * HALF, HALF)
        n = w * NX + xp(2)
        return (term[n, rows].astype(F32) + term_in[n, rows].astype(F32)).astype(BF16)

    for w in range(2):
        for d in range(2):
            x1_out[d, w] = far_half(w, d)
    b_x1 = [send(x1_out.at[d], x1_in.at[d], b_send.at[1 + d], b_recv.at[1 + d], (right, left)[d]) for d in range(2)]

    finish(1, 1 - hi, *f_far)
    for copy in a_s:
        copy.wait_recv()

    def product(dest, piece):
        return jnp.dot(acts_ref[...], weight[2 * dest + piece], preferred_element_type=F32)

    def send_c(n, dest, piece, peer, prior):
        value = product(dest, piece)
        if prior is not None:
            k, copy = prior
            copy.wait_recv()
            value = value + y_in[k].astype(F32)
        y_out[n] = value.astype(BF16)
        return n, send(y_out.at[n], y_in.at[n], c_send.at[n], c_recv.at[n], peer)

    up0 = send_c(0, yp(4), 0, up, None)
    dn1 = send_c(7, yp(-4), 1, down, None)
    up1 = send_c(1, yp(3), 1, up, None)
    dn0 = send_c(8, yp(-3), 0, down, None)

    acc[...] = jnp.zeros_like(acc)

    def grad_block(n, carry):
        acc[...] += lax.dot_general(
            scaled[n], weight[n], (((1,), (1,)), ((), ())), preferred_element_type=F32
        )
        return carry

    lax.fori_loop(0, NO, grad_block, 0)
    act_grad_ref[...] = acc[...].astype(BF16)

    up0 = send_c(2, yp(3), 0, up, up0)
    dn1 = send_c(9, yp(-3), 1, down, dn1)

    for d in range(2):
        b_x1[d].wait_recv()
    for d in range(2):
        near = xp(1 - 2 * d)
        other = pl.ds((1 - d) * HALF, HALF)
        rows = pl.ds(d * HALF, HALF)
        for w in range(2):
            n = w * NX + near
            x2_out[d, w, other] = (term[n, other].astype(F32) + term_in[n, other].astype(F32)).astype(BF16)
            x2_out[d, w, rows] = (
                term[n, rows].astype(F32) + term_in[n, rows].astype(F32) + x1_in[d, w].astype(F32)
            ).astype(BF16)
    b_x2 = [send(x2_out.at[d], x2_in.at[d], b_send.at[3 + d], b_recv.at[3 + d], (right, left)[d]) for d in range(2)]

    up1 = send_c(3, yp(2), 1, up, up1)
    dn0 = send_c(10, yp(-2), 0, down, dn0)
    up0 = send_c(4, yp(2), 0, up, up0)
    dn1 = send_c(11, yp(-2), 1, down, dn1)

    for d in range(2):
        b_x2[d].wait_recv()

    def reduced(w):
        n = w * NX + x
        return (
            term[n].astype(F32) + term_in[n].astype(F32) + x2_in[0, w].astype(F32) + x2_in[1, w].astype(F32)
        )

    z_out[...] = reduced(1 - hi).astype(BF16)
    b_z = send(z_out, z_in, b_send.at[5], b_recv.at[5], partner)

    up1 = send_c(5, yp(1), 1, up, up1)
    dn0 = send_c(12, yp(-1), 0, down, dn0)
    up0 = send_c(6, yp(1), 0, up, up0)
    dn1 = send_c(13, yp(-1), 1, down, dn1)

    wgrad_ref[...] = reduced(hi)

    for piece in range(2):
        value = product(y, piece)
        for k, copy in ((up0, dn0), (up1, dn1))[piece]:
            copy.wait_recv()
            value = value + y_in[k].astype(F32)
        for b in range(3):
            n = 3 * piece + b
            part = value[:, b * 128 : (b + 1) * 128]
            m_own[n] = part
            m_out[n] = part.astype(BF16)

            @pl.when(z != n)
            def _():
                pltpu.make_async_remote_copy(
                    src_ref=m_out.at[n], dst_ref=m_in.at[z], send_sem=m_send.at[n], recv_sem=m_recv.at[z],
                    device_id=(o, y * NZ + n), device_id_type=MESH,
                ).start()

    b_z.wait_recv()
    wgrad_ref[...] += z_in[...].astype(F32)

    acc[:, :128] = m_own[z]
    for n in range(NZ):

        @pl.when(z != n)
        def _():
            copy = pltpu.make_async_remote_copy(
                src_ref=m_out.at[n], dst_ref=m_in.at[n], send_sem=m_send.at[n], recv_sem=m_recv.at[n],
                device_id=(o, y * NZ + n), device_id_type=MESH,
            )
            copy.wait_recv()
            acc[:, :128] += m_in[n].astype(F32)
            copy.wait_send()

    mixed_ref[...] = (coef[...] * acc[:, :128]).astype(BF16)
    for copy in sent:
        copy.wait_send()


def local(acts, codes, scales, routes, route_logits, cotangent):
    vmem = pl.BlockSpec(memory_space=pltpu.VMEM)
    dma = pltpu.SemaphoreType.DMA
    blk = (FFD, COLS)
    return tuple(
        pl.pallas_call(
            kernel,
            name="expert_down",
            out_shape=(
                jax.ShapeDtypeStruct((TOK, 128), BF16),
                jax.ShapeDtypeStruct((TOK, FFD), BF16),
                jax.ShapeDtypeStruct(blk, F32),
            ),
            in_specs=[vmem] * 6,
            out_specs=[vmem] * 3,
            scratch_shapes=[
                pltpu.VMEM((NO, *blk), BF16),
                pltpu.VMEM((NO, TOK, COLS), BF16),
                pltpu.VMEM((TOK, 1), F32),
                pltpu.VMEM((FFD, TOK), BF16),
                pltpu.VMEM((8, *blk), BF16),
                pltpu.VMEM((8, *blk), BF16),
                pltpu.VMEM((8, *blk), BF16),
                pltpu.VMEM((2, 2, HALF, COLS), BF16),
                pltpu.VMEM((2, 2, HALF, COLS), BF16),
                pltpu.VMEM((2, 2, *blk), BF16),
                pltpu.VMEM((2, 2, *blk), BF16),
                pltpu.VMEM(blk, BF16),
                pltpu.VMEM(blk, BF16),
                pltpu.VMEM((N_C, TOK, COLS), BF16),
                pltpu.VMEM((N_C, TOK, COLS), BF16),
                pltpu.VMEM((NZ, TOK, 128), F32),
                pltpu.VMEM((NZ, TOK, 128), BF16),
                pltpu.VMEM((NZ, TOK, 128), BF16),
                pltpu.VMEM((TOK, FFD), F32),
                dma((N_A,)), dma((N_A,)), dma((N_B,)), dma((N_B,)),
                dma((N_C,)), dma((N_C,)), dma((NZ,)), dma((NZ,)),
            ],
            compiler_params=pltpu.CompilerParams(
                collective_id=0, has_side_effects=True, vmem_limit_bytes=48 * 2**20
            ),
            cost_estimate=pl.CostEstimate(flops=2_500_000_000, bytes_accessed=8_000_000, transcendentals=0),
        )(acts, codes, scales.T, routes, route_logits, cotangent)
    )


def solution(mesh):
    in_specs = (
        P("outer", "inner"),
        P("inner", "outer"),
        P("outer", "inner"),
        P("outer", None),
        P("outer", None),
        P("outer", None),
    )
    out_specs = (P("outer", "inner"), P("outer", "inner"), P("inner", "outer"))
    return jax.shard_map(local, mesh=mesh, in_specs=in_specs, out_specs=out_specs, check_vma=False)
```

time: 574 us -> 97.3 us (0.17)
  the two profiles are of different devices: /device:TPU:6 before, /device:TPU:67 now
where the time goes in v1:
time: 97.3 us; the launch traced here: 97 us
  Pallas kernels  88.1 us (91%)
  local copies, waits for them, and re-layouts  8.19 us (8%)
    pallas_call x1, Pallas kernels, local(): pl.pallas_call(kernel, name='expert_down', out_shape=(jax.ShapeDtypeStruc...  88.1 us
    unnamed x12, local copies, waits for them, and re-layouts  8.19 us

profile of v1, /device:TPU:67, one launch (start us, length us, event | category | flops | bytes accessed | tf_op | source)
XLA Modules:
  0.0 97.0 jit_solution(1417502538703481944)
XLA Ops:
  0.6 0.8 copy.9
  1.5 0.8 copy.10.routes_ref
  2.3 0.8 copy.11.logits_ref
  3.1 0.0 copy-start
  3.1 1.9 %copy-done = bf16[256,6144]{1,0:T(8,128)(2,1)S(1)} copy-done((bf16[256,6144]{1,0:T(8,128)(2,1)S(1)}, bf16[256,6144]{1,0:T(8,128)(2,1)}, u32[]{:S(2)}) %copy-start) | copy-done | bytes 3145752
  5.0 0.0 copy-start.1
  5.0 0.9 copy-done.1
  5.9 0.0 copy-start.2
  5.9 0.9 copy-done.2
  6.8 88.1 %expert_down.1 = (bf16[256,128]{1,0:T(8,128)(2,1)S(1)}, bf16[256,256]{1,0:T(8,128)(2,1)S(1)}, f32[256,384]{1,0:T(8,128)S(1)}) custom-call(bf16[256,256]{1,0:T(8,128)(2,1)S(1)} %copy-done.2, bf16[256,384]{1,0:T(8,128)(2,1)S(1)} %copy-done.1, f32[256,3]{1,0:T(8,128)S(1)} %bitcast.1, s32[256,2]{1,0:T(8,128)S(1)} %copy.10.routes_ref, ...), custom_call_target="tpu_custom_call" | custom-call | flops 2500000000 | bytes 8000000 | tf_op jit(solution)/shard_map/expert_down/pallas_call | solution.py:271
  94.9 0.6 copy.15
  95.6 0.7 copy.16
  96.2 0.7 copy.17
Async XLA Ops:
  3.1 1.9 %copy-start = (bf16[256,6144]{1,0:T(8,128)(2,1)S(1)}, bf16[256,6144]{1,0:T(8,128)(2,1)}, u32[]{:S(2)}) copy-start(bf16[256,6144]{1,0:T(8,128)(2,1)} %cot_ref.1) | copy-start | bytes 9437188
  5.0 0.9 copy-start.1
  5.9 0.9 copy-start.2

commit v2 on v0

v2 whole, which is shorter than its diff:
```python
import jax
import jax.numpy as jnp
from jax import lax
from jax.experimental import pallas as pl
from jax.experimental.pallas import tpu as pltpu
from jax.sharding import PartitionSpec as P

MESH = pl.DeviceIdType.MESH
BF16 = jnp.bfloat16
F32 = jnp.float32
NX, NY, NZ = 4, 8, 6
TOK, FFD, COLS = 256, 256, 384
HALF = FFD // 2
NS = 3
N_HOP, N_COPY = 14 * NS, 88


def kernel(
    acts_ref, codes_ref, scales_ref, routes_ref, logits_ref, cot_ref,
    mixed_ref, act_grad_ref, wgrad_ref,
    acts_v, codes_v, scales_v, routes_v, logits_v, cot_v,
    weight, scaled, coef, acts_t, term_out, term_in, term,
    x1_out, x1_in, x2_out, x2_in, z_out, z_in,
    prod, y_out, y_in, m_own, m_out, m_in, acc,
    in_sem, s_sem, r_sem, m_send, m_recv,
):
    o = lax.axis_index("outer")
    i = lax.axis_index("inner")
    core = lax.rem(o, 2)
    chip = lax.div(o, 2)
    x = lax.rem(chip, NX)
    hi = lax.div(chip, NX)
    y = lax.div(i, NZ)
    z = lax.rem(i, NZ)

    def xp(n):
        return lax.rem(x + n + NX, NX)

    def yp(n):
        return lax.rem(y + n + NY, NY)

    sibling = (chip * 2 + 1 - core, i)
    partner = (((1 - hi) * NX + x) * 2 + core, i)
    right, left = ((hi * NX + xp(1)) * 2 + core, i), ((hi * NX + xp(-1)) * 2 + core, i)
    up, down = (o, yp(1) * NZ + z), (o, yp(-1) * NZ + z)

    def load(n, src, dst):
        copy = pltpu.make_async_copy(src, dst, in_sem.at[n])
        copy.start()
        return copy

    scales_v[...] = jnp.zeros_like(scales_v)
    loads = [
        load(0, scales_ref, scales_v.at[pl.ds(0, 3)]),
        load(1, codes_ref, codes_v),
        load(2, routes_ref, routes_v),
        load(3, logits_ref, logits_v),
        load(4, acts_ref, acts_v),
        load(5, cot_ref, cot_v),
    ]

    barrier = pltpu.get_barrier_semaphore()
    for peer in (sibling, partner, right, left, up, down):
        pl.semaphore_signal(barrier, inc=1, device_id=peer, device_id_type=MESH)
    for n in range(1, NZ):
        pl.semaphore_signal(barrier, inc=1, device_id=(o, y * NZ + lax.rem(z + n, NZ)), device_id_type=MESH)

    loads[0].wait()
    factors = scales_v[...].T
    loads[1].wait()
    for b in range(NS):
        cols = pl.ds(b * 128, 128)
        weight[chip, core, b] = (codes_v[:, cols].astype(F32) * factors[:, b : b + 1]).astype(BF16)
    pl.semaphore_wait(barrier, 6 + NZ - 1)

    sent = []

    def send(src, dst, peer):
        n = len(sent)
        copy = pltpu.make_async_remote_copy(
            src_ref=src, dst_ref=dst, send_sem=s_sem.at[n], recv_sem=r_sem.at[n],
            device_id=peer, device_id_type=MESH,
        )
        copy.start()
        sent.append(copy)
        return copy

    def same(ref, peer):
        return send(ref, ref, peer)

    far = 1 - hi
    far_z = [same(weight.at[chip, core, b], partner) for b in range(NS)]
    own = weight.at[chip, core]
    own_r, own_l = same(own, right), same(own, left)
    own_shared = [same(own, sibling)]

    loads[2].wait()
    loads[3].wait()
    lg = logits_v[...]
    ex = jnp.exp(lg - jnp.max(lg, axis=0, keepdims=True))
    probs = ex / jnp.sum(ex, axis=0, keepdims=True)
    row = jnp.sum(probs * (routes_v[...] == 0).astype(F32), axis=0, keepdims=True)
    coef[...] = jnp.broadcast_to(row, (8, TOK)).T[:, :1]
    loads[4].wait()
    acts_t[...] = acts_v[...].T
    loads[5].wait()

    def scale_chip(k, carry):
        for c in range(2):
            for b in range(NS):
                cols = pl.ds(pl.multiple_of(k * (2 * COLS), 128) + (c * COLS + b * 128), 128)
                scaled[k, c, b] = (coef[...] * cot_v[:, cols].astype(F32)).astype(BF16)
        return carry

    lax.fori_loop(0, NY, scale_chip, 0)

    def own_near():
        own_r.wait_recv()
        w = weight.at[hi * NX + xp(-1), core]
        f_r = same(w.at[:, pl.ds(0, HALF)], right)
        own_shared.append(same(w, sibling))
        own_l.wait_recv()
        w = weight.at[hi * NX + xp(1), core]
        f_l = same(w.at[:, pl.ds(HALF, HALF)], left)
        own_shared.append(same(w, sibling))
        return f_r, f_l

    own_f = own_near()

    def terms(dst, c):
        def body(k, carry):
            g = jnp.concatenate([scaled[k, c, b] for b in range(NS)], axis=1)
            dst[k] = jnp.dot(acts_t[...], g, preferred_element_type=F32).astype(BF16)
            return carry

        lax.fori_loop(0, NY, body, 0)

    terms(term_out, 1 - core)
    b_pair = send(term_out, term_in, sibling)

    for copy in own_f:
        copy.wait_recv()
    own_shared.append(same(weight.at[hi * NX + xp(2), core], sibling))

    far_x, far_f, far_shared = [None] * NS, [None] * NS, [[] for _ in range(NS)]

    def far_1(b):
        far_z[b].wait_recv()
        w = weight.at[far * NX + x, core, b]
        far_x[b] = same(w, right), same(w, left)
        far_shared[b].append(same(w, sibling))

    def far_2(b):
        far_x[b][0].wait_recv()
        w = weight.at[far * NX + xp(-1), core, b]
        f_r = same(w.at[pl.ds(0, HALF)], right)
        far_shared[b].append(same(w, sibling))
        far_x[b][1].wait_recv()
        w = weight.at[far * NX + xp(1), core, b]
        f_l = same(w.at[pl.ds(HALF, HALF)], left)
        far_shared[b].append(same(w, sibling))
        far_f[b] = f_r, f_l

    def far_3(b):
        for copy in far_f[b]:
            copy.wait_recv()
        far_shared[b].append(same(weight.at[far * NX + xp(2), core, b], sibling))

    def far_4(b):
        if b == 0:
            for copy in own_shared:
                copy.wait_recv()
        for copy in far_shared[b]:
            copy.wait_recv()

    b_x1, b_x2, b_z = [], [], []

    def paired(n, rows):
        return term[n, rows].astype(F32) + term_in[n, rows].astype(F32)

    def half(d):
        return pl.ds(d * HALF, HALF)

    def grad_1():
        b_pair.wait_recv()
        for d in range(2):
            for w in range(2):
                x1_out[d, w] = paired(w * NX + xp(2), half(d)).astype(BF16)
            b_x1.append(send(x1_out.at[d], x1_in.at[d], (right, left)[d]))

    def grad_2():
        for d in range(2):
            for w in range(2):
                n = w * NX + xp(1 - 2 * d)
                x2_out[d, w, half(1 - d)] = paired(n, half(1 - d)).astype(BF16)
        for d in range(2):
            b_x1[d].wait_recv()
            for w in range(2):
                n = w * NX + xp(1 - 2 * d)
                x2_out[d, w, half(d)] = (paired(n, half(d)) + x1_in[d, w].astype(F32)).astype(BF16)
            b_x2.append(send(x2_out.at[d], x2_in.at[d], (right, left)[d]))

    def reduced(w):
        return paired(w * NX + x, pl.ds(0, FFD)) + x2_in[0, w].astype(F32) + x2_in[1, w].astype(F32)

    def grad_3():
        for copy in b_x2:
            copy.wait_recv()
        z_out[...] = reduced(far).astype(BF16)
        b_z.append(send(z_out, z_in, partner))
        wgrad_ref[...] = reduced(hi)

    chains = [{} for _ in range(NS)]

    def product(b, slot, dest):
        w = jnp.concatenate([weight[dest, 0, b], weight[dest, 1, b]], axis=1)
        prod[slot] = jnp.dot(acts_v[...], w, preferred_element_type=F32)

    def hop(b, way, h, slot):
        prior = chains[b].get((way, h))
        value = prod[slot, half(h)]
        if prior is not None:
            n, copy = prior
            copy.wait_recv()
            value = value + y_in[n].astype(F32)
        n = hop.count
        hop.count += 1
        y_out[n] = value.astype(BF16)
        chains[b][(way, h)] = n, send(y_out.at[n], y_in.at[n], (up, down)[way])

    hop.count = 0

    def tick(b, t):
        p_up, p_down = 2 * b, 2 * b + 1
        if t == 0:
            product(b, p_up, yp(4))
            hop(b, 0, 0, p_up)
            hop(b, 1, 1, p_up)
            return
        d = 3 - (t - 1) // 2
        if t == 7:
            product(b, p_up, y)
            for h in range(2):
                value = prod[p_up, half(h)]
                for way in range(2):
                    n, copy = chains[b][(way, h)]
                    copy.wait_recv()
                    value = value + y_in[n].astype(F32)
                for c in range(2):
                    part = value[:, c * 128 : (c + 1) * 128]
                    m_own[3 * c + b, half(h)] = part
                    m_out[3 * c + b, half(h)] = part.astype(BF16)
            for c in range(2):
                n = 3 * c + b

                @pl.when(z != n)
                def _():
                    pltpu.make_async_remote_copy(
                        src_ref=m_out.at[n], dst_ref=m_in.at[z], send_sem=m_send.at[n], recv_sem=m_recv.at[z],
                        device_id=(o, y * NZ + n), device_id_type=MESH,
                    ).start()
            return
        if t % 2 == 1:
            product(b, p_up, yp(d))
            product(b, p_down, yp(-d))
            hop(b, 0, 1, p_up)
            hop(b, 1, 0, p_down)
        else:
            hop(b, 0, 0, p_up)
            hop(b, 1, 1, p_down)

    far_1(0)
    terms(term, core)
    far_2(0)
    far_1(1)
    far_3(0)
    far_2(1)
    far_1(2)
    grad_1()
    far_3(1)
    far_4(0)
    tick(0, 0)
    tick(0, 1)
    far_2(2)
    tick(0, 2)
    far_3(2)
    grad_2()
    far_4(1)
    tick(1, 0)
    tick(0, 3)
    tick(1, 1)
    tick(0, 4)
    far_4(2)
    tick(1, 2)
    tick(2, 0)
    tick(0, 5)
    tick(1, 3)
    tick(2, 1)
    grad_3()
    tick(0, 6)
    tick(1, 4)
    tick(2, 2)
    tick(0, 7)
    tick(1, 5)
    tick(2, 3)
    tick(1, 6)
    tick(2, 4)
    tick(1, 7)
    tick(2, 5)
    tick(2, 6)
    tick(2, 7)

    acc[...] = jnp.zeros_like(acc)

    def act_block(k, carry):
        total = acc[...]
        for b in range(NS):
            g = jnp.concatenate([scaled[k, 0, b], scaled[k, 1, b]], axis=1)
            w = jnp.concatenate([weight[k, 0, b], weight[k, 1, b]], axis=1)
            total += lax.dot_general(g, w, (((1,), (1,)), ((), ())), preferred_element_type=F32)
        acc[...] = total
        return carry

    lax.fori_loop(0, NY, act_block, 0)
    act_grad_ref[...] = acc[...].astype(BF16)

    b_z[0].wait_recv()
    wgrad_ref[...] += z_in[...].astype(F32)

    acc[:, :128] = m_own[z]
    for n in range(NZ):

        @pl.when(z != n)
        def _():
            copy = pltpu.make_async_remote_copy(
                src_ref=m_out.at[n], dst_ref=m_in.at[n], send_sem=m_send.at[n], recv_sem=m_recv.at[n],
                device_id=(o, y * NZ + n), device_id_type=MESH,
            )
            copy.wait_recv()
            acc[:, :128] += m_in[n].astype(F32)
            copy.wait_send()

    mixed_ref[...] = (coef[...] * acc[:, :128]).astype(BF16)
    for copy in sent:
        copy.wait_send()


def local(acts, codes, scales, routes, route_logits, cotangent):
    vmem = pl.BlockSpec(memory_space=pltpu.VMEM)
    dma = pltpu.SemaphoreType.DMA
    blk = (FFD, COLS)
    return tuple(
        pl.pallas_call(
            kernel,
            name="expert_down",
            out_shape=(
                jax.ShapeDtypeStruct((TOK, 128), BF16),
                jax.ShapeDtypeStruct((TOK, FFD), BF16),
                jax.ShapeDtypeStruct(blk, F32),
            ),
            in_specs=[pl.BlockSpec(memory_space=pltpu.HBM)] * 6,
            out_specs=[vmem] * 3,
            scratch_shapes=[
                pltpu.VMEM((TOK, FFD), BF16),
                pltpu.VMEM(blk, BF16),
                pltpu.VMEM((8, FFD), F32),
                pltpu.VMEM((2, TOK), jnp.int32),
                pltpu.VMEM((2, TOK), F32),
                pltpu.VMEM((TOK, 16 * COLS), BF16),
                pltpu.VMEM((NY, 2, NS, FFD, 128), BF16),
                pltpu.VMEM((NY, 2, NS, TOK, 128), BF16),
                pltpu.VMEM((TOK, 1), F32),
                pltpu.VMEM((FFD, TOK), BF16),
                pltpu.VMEM((NY, *blk), BF16),
                pltpu.VMEM((NY, *blk), BF16),
                pltpu.VMEM((NY, *blk), BF16),
                pltpu.VMEM((2, 2, HALF, COLS), BF16),
                pltpu.VMEM((2, 2, HALF, COLS), BF16),
                pltpu.VMEM((2, 2, *blk), BF16),
                pltpu.VMEM((2, 2, *blk), BF16),
                pltpu.VMEM(blk, BF16),
                pltpu.VMEM(blk, BF16),
                pltpu.VMEM((2 * NS, TOK, 256), F32),
                pltpu.VMEM((N_HOP, HALF, 256), BF16),
                pltpu.VMEM((N_HOP, HALF, 256), BF16),
                pltpu.VMEM((NZ, TOK, 128), F32),
                pltpu.VMEM((NZ, TOK, 128), BF16),
                pltpu.VMEM((NZ, TOK, 128), BF16),
                pltpu.VMEM((TOK, FFD), F32),
                dma((6,)), dma((N_COPY,)), dma((N_COPY,)), dma((NZ,)), dma((NZ,)),
            ],
            compiler_params=pltpu.CompilerParams(
                collective_id=0, has_side_effects=True, vmem_limit_bytes=36 * 2**20
            ),
            cost_estimate=pl.CostEstimate(flops=2_500_000_000, bytes_accessed=8_000_000, transcendentals=0),
        )(*(pltpu.with_memory_space_constraint(a, pltpu.HBM) for a in (acts, codes, scales, routes.T, route_logits.T, cotangent)))
    )


def solution(mesh):
    in_specs = (
        P("outer", "inner"),
        P("inner", "outer"),
        P("outer", "inner"),
        P("outer", None),
        P("outer", None),
        P("outer", None),
    )
    out_specs = (P("outer", "inner"), P("outer", "inner"), P("inner", "outer"))
    return jax.shard_map(local, mesh=mesh, in_specs=in_specs, out_specs=out_specs, check_vma=False)
```

time: 574 us -> 84.2 us (0.15)
  waiting for transfers between devices: 499 us -> 0 us
  Pallas kernels: 0 us -> 81.2 us
  blocking collectives: 33.3 us -> 0 us
  matrix products: 17.3 us -> 0 us
  between operations: 13.8 us -> 0.64 us
    reduce_scatter x2 -> x0, waiting for transfers between devices: 435 us -> none  [the longest x1 320 us: local(): lax.psum_scatter(partial_value, 'inner', scatter_dimension=1, tiled=True)]
    pallas_call x0 -> x1, Pallas kernels: none -> 81.2 us  [local(): pl.pallas_call(kernel, name='expert_down', out_shape=(jax.ShapeDtypeStruc...]
    all_gather x1 -> x0, waiting for transfers between devices: 63.4 us -> none  [local(): lax.all_gather(codes, 'outer', axis=1, tiled=True)]
    all_gather x1 -> x0, blocking collectives: 33.3 us -> none  [local(): lax.all_gather(scales.astype(jnp.bfloat16), 'outer', axis=0, tiled=True)]
    dot_general x3 -> x0, matrix products: 17.3 us -> none  [the longest x1 6.63 us: local(): lax.dot_general(scaled, weight, (((1,), (1,)), ((), ())), preferred_eleme...]
  transfers between devices with their start and end apart: 3 -> 0, of which waited for: 3 -> 0; matrix products, arithmetic and copies ran while one was open for 4% -> 0% of each run, Pallas kernels for 0% -> 0%
where the time goes in v2:
time: 84.2 us; the launch traced here: 83.9 us
  Pallas kernels  81.2 us (96%)
  local copies, waits for them, and re-layouts  2.03 us (2%)
    pallas_call x1, Pallas kernels, local(): pl.pallas_call(kernel, name='expert_down', out_shape=(jax.ShapeDtypeStruc...  81.2 us
    unnamed x3, local copies, waits for them, and re-layouts  2.03 us

profile of v2, /device:TPU:6, one launch (start us, length us, event | category | flops | bytes accessed | tf_op | source)
XLA Modules:
  0.0 83.9 jit_solution(16501240157519798537)
XLA Ops:
  0.6 81.2 %expert_down.1 = (bf16[256,128]{1,0:T(8,128)(2,1)S(1)}, bf16[256,256]{1,0:T(8,128)(2,1)S(1)}, f32[256,384]{1,0:T(8,128)S(1)}) custom-call(bf16[256,256]{1,0:T(8,128)(2,1)} %acts_ref.1, bf16[256,384]{1,0:T(8,128)(2,1)} %codes_ref.1, f32[3,256]{1,0:T(4,128)} %scales_ref.1, s32[2,256]{1,0:T(2,128)} %bitcast.2, f32[2,256]{1,0:T(2,128)} %bitcast.3, ...), custom_call_target="tpu_custom_call" | custom-call | flops 2500000000 | bytes 8000000 | tf_op jit(solution)/shard_map/expert_down/pallas_call | solution.py:353
  81.8 0.6 copy.12
  82.5 0.7 copy.13
  83.1 0.7 copy.14

commit v3 on v2

--- a/solution.py
+++ b/solution.py
@@ -42,6 +42,7 @@
     sibling = (chip * 2 + 1 - core, i)
     partner = (((1 - hi) * NX + x) * 2 + core, i)
     right, left = ((hi * NX + xp(1)) * 2 + core, i), ((hi * NX + xp(-1)) * 2 + core, i)
+    across = ((hi * NX + xp(2)) * 2 + core, i)
     up, down = (o, yp(1) * NZ + z), (o, yp(-1) * NZ + z)
 
     def load(n, src, dst):
@@ -60,7 +61,7 @@
     ]
 
     barrier = pltpu.get_barrier_semaphore()
-    for peer in (sibling, partner, right, left, up, down):
+    for peer in (sibling, partner, right, left, across, up, down):
         pl.semaphore_signal(barrier, inc=1, device_id=peer, device_id_type=MESH)
     for n in range(1, NZ):
         pl.semaphore_signal(barrier, inc=1, device_id=(o, y * NZ + lax.rem(z + n, NZ)), device_id_type=MESH)
@@ -71,7 +72,7 @@
     for b in range(NS):
         cols = pl.ds(b * 128, 128)
         weight[chip, core, b] = (codes_v[:, cols].astype(F32) * factors[:, b : b + 1]).astype(BF16)
-    pl.semaphore_wait(barrier, 6 + NZ - 1)
+    pl.semaphore_wait(barrier, 7 + NZ - 1)
 
     sent = []
 
@@ -91,7 +92,7 @@
     far = 1 - hi
     far_z = [same(weight.at[chip, core, b], partner) for b in range(NS)]
     own = weight.at[chip, core]
-    own_r, own_l = same(own, right), same(own, left)
+    own_x = [same(own, peer) for peer in (right, left, across)]
     own_shared = [same(own, sibling)]
 
     loads[2].wait()
@@ -115,17 +116,11 @@
     lax.fori_loop(0, NY, scale_chip, 0)
 
     def own_near():
-        own_r.wait_recv()
-        w = weight.at[hi * NX + xp(-1), core]
-        f_r = same(w.at[:, pl.ds(0, HALF)], right)
-        own_shared.append(same(w, sibling))
-        own_l.wait_recv()
-        w = weight.at[hi * NX + xp(1), core]
-        f_l = same(w.at[:, pl.ds(HALF, HALF)], left)
-        own_shared.append(same(w, sibling))
-        return f_r, f_l
-
-    own_f = own_near()
+        for copy, n in zip(own_x, (-1, 1, 2)):
+            copy.wait_recv()
+            own_shared.append(same(weight.at[hi * NX + xp(n), core], sibling))
+
+    own_near()
 
     def terms(dst, c):
         def body(k, carry):
@@ -138,33 +133,18 @@
     terms(term_out, 1 - core)
     b_pair = send(term_out, term_in, sibling)
 
-    for copy in own_f:
-        copy.wait_recv()
-    own_shared.append(same(weight.at[hi * NX + xp(2), core], sibling))
-
-    far_x, far_f, far_shared = [None] * NS, [None] * NS, [[] for _ in range(NS)]
+    far_x, far_shared = [None] * NS, [[] for _ in range(NS)]
 
     def far_1(b):
         far_z[b].wait_recv()
         w = weight.at[far * NX + x, core, b]
-        far_x[b] = same(w, right), same(w, left)
+        far_x[b] = [same(w, peer) for peer in (right, left, across)]
         far_shared[b].append(same(w, sibling))
 
     def far_2(b):
-        far_x[b][0].wait_recv()
-        w = weight.at[far * NX + xp(-1), core, b]
-        f_r = same(w.at[pl.ds(0, HALF)], right)
-        far_shared[b].append(same(w, sibling))
-        far_x[b][1].wait_recv()
-        w = weight.at[far * NX + xp(1), core, b]
-        f_l = same(w.at[pl.ds(HALF, HALF)], left)
-        far_shared[b].append(same(w, sibling))
-        far_f[b] = f_r, f_l
-
-    def far_3(b):
-        for copy in far_f[b]:
-            copy.wait_recv()
-        far_shared[b].append(same(weight.at[far * NX + xp(2), core, b], sibling))
+        for copy, n in zip(far_x[b], (-1, 1, 2)):
+            copy.wait_recv()
+            far_shared[b].append(same(weight.at[far * NX + xp(n), core, b], sibling))
 
     def far_4(b):
         if b == 0:
@@ -183,31 +163,36 @@
 
     def grad_1():
         b_pair.wait_recv()
-        for d in range(2):
-            for w in range(2):
+        for w in (far, hi):
+            for d in range(2):
                 x1_out[d, w] = paired(w * NX + xp(2), half(d)).astype(BF16)
-            b_x1.append(send(x1_out.at[d], x1_in.at[d], (right, left)[d]))
+                b_x1.append(send(x1_out.at[d, w], x1_in.at[d, w], (right, left)[d]))
 
     def grad_2():
         for d in range(2):
             for w in range(2):
                 n = w * NX + xp(1 - 2 * d)
                 x2_out[d, w, half(1 - d)] = paired(n, half(1 - d)).astype(BF16)
-        for d in range(2):
-            b_x1[d].wait_recv()
-            for w in range(2):
+        for k in range(2):
+            w = (far, hi)[k]
+            for d in range(2):
+                b_x1[2 * k + d].wait_recv()
                 n = w * NX + xp(1 - 2 * d)
                 x2_out[d, w, half(d)] = (paired(n, half(d)) + x1_in[d, w].astype(F32)).astype(BF16)
-            b_x2.append(send(x2_out.at[d], x2_in.at[d], (right, left)[d]))
+                b_x2.append(send(x2_out.at[d, w], x2_in.at[d, w], (right, left)[d]))
 
     def reduced(w):
         return paired(w * NX + x, pl.ds(0, FFD)) + x2_in[0, w].astype(F32) + x2_in[1, w].astype(F32)
 
     def grad_3():
-        for copy in b_x2:
+        for copy in b_x2[:2]:
             copy.wait_recv()
         z_out[...] = reduced(far).astype(BF16)
         b_z.append(send(z_out, z_in, partner))
+
+    def grad_4():
+        for copy in b_x2[2:]:
+            copy.wait_recv()
         wgrad_ref[...] = reduced(hi)
 
     chains = [{} for _ in range(NS)]
@@ -269,28 +254,37 @@
             hop(b, 0, 0, p_up)
             hop(b, 1, 1, p_down)
 
+    def act_block(k):
+        total = acc[...] if k else None
+        for b in range(NS):
+            g = jnp.concatenate([scaled[k, 0, b], scaled[k, 1, b]], axis=1)
+            w = jnp.concatenate([weight[k, 0, b], weight[k, 1, b]], axis=1)
+            part = lax.dot_general(g, w, (((1,), (1,)), ((), ())), preferred_element_type=F32)
+            total = part if total is None else total + part
+        if k < NY - 1:
+            acc[...] = total
+        else:
+            act_grad_ref[...] = total.astype(BF16)
+
     far_1(0)
     terms(term, core)
+    far_1(1)
     far_2(0)
-    far_1(1)
-    far_3(0)
+    far_1(2)
     far_2(1)
-    far_1(2)
+    far_4(0)
     grad_1()
-    far_3(1)
-    far_4(0)
     tick(0, 0)
     tick(0, 1)
     far_2(2)
+    far_4(1)
     tick(0, 2)
-    far_3(2)
+    tick(1, 0)
     grad_2()
-    far_4(1)
-    tick(1, 0)
     tick(0, 3)
     tick(1, 1)
+    far_4(2)
     tick(0, 4)
-    far_4(2)
     tick(1, 2)
     tick(2, 0)
     tick(0, 5)
@@ -302,28 +296,23 @@
     tick(2, 2)
     tick(0, 7)
     tick(1, 5)
+    act_block(0)
     tick(2, 3)
+    act_block(1)
     tick(1, 6)
+    act_block(2)
     tick(2, 4)
+    act_block(3)
     tick(1, 7)
+    act_block(4)
     tick(2, 5)
+    act_block(5)
     tick(2, 6)
+    act_block(6)
     tick(2, 7)
-
-    acc[...] = jnp.zeros_like(acc)
-
-    def act_block(k, carry):
-        total = acc[...]
-        for b in range(NS):
-            g = jnp.concatenate([scaled[k, 0, b], scaled[k, 1, b]], axis=1)
-            w = jnp.concatenate([weight[k, 0, b], weight[k, 1, b]], axis=1)
-            total += lax.dot_general(g, w, (((1,), (1,)), ((), ())), preferred_element_type=F32)
-        acc[...] = total
-        return carry
-
-    lax.fori_loop(0, NY, act_block, 0)
-    act_grad_ref[...] = acc[...].astype(BF16)
-
+    act_block(7)
+
+    grad_4()
     b_z[0].wait_recv()
     wgrad_ref[...] += z_in[...].astype(F32)
 

time: 84.2 us -> 82.3 us (0.977); the launches traced: 83.9 us -> 80.8 us
  Pallas kernels: 81.2 us -> 78.1 us
    pallas_call x1, Pallas kernels: 81.2 us -> 78.1 us  [local(): pl.pallas_call(kernel, name='expert_down', out_shape=(jax.ShapeDtypeStruc...]
where the time goes in v3:
time: 82.3 us; the launch traced here: 80.8 us
  Pallas kernels  78.1 us (95%)
  local copies, waits for them, and re-layouts  2.03 us (2%)
    pallas_call x1, Pallas kernels, local(): pl.pallas_call(kernel, name='expert_down', out_shape=(jax.ShapeDtypeStruc...  78.1 us
    unnamed x3, local copies, waits for them, and re-layouts  2.03 us

profile of v3, /device:TPU:6, one launch (start us, length us, event | category | flops | bytes accessed | tf_op | source)
XLA Modules:
  0.0 80.8 jit_solution(18287229151688979518)
XLA Ops:
  0.6 78.1 %expert_down.1 = (bf16[256,128]{1,0:T(8,128)(2,1)S(1)}, bf16[256,256]{1,0:T(8,128)(2,1)S(1)}, f32[256,384]{1,0:T(8,128)S(1)}) custom-call(bf16[256,256]{1,0:T(8,128)(2,1)} %acts_ref.1, bf16[256,384]{1,0:T(8,128)(2,1)} %codes_ref.1, f32[3,256]{1,0:T(4,128)} %scales_ref.1, s32[2,256]{1,0:T(2,128)} %bitcast.2, f32[2,256]{1,0:T(2,128)} %bitcast.3, ...), custom_call_target="tpu_custom_call" | custom-call | flops 2500000000 | bytes 8000000 | tf_op jit(solution)/shard_map/expert_down/pallas_call | solution.py:342
  78.8 0.6 copy.12
  79.4 0.7 copy.13
  80.0 0.7 copy.14

commit v4 on v3

--- a/solution.py
+++ b/solution.py
@@ -92,7 +92,7 @@
     far = 1 - hi
     far_z = [same(weight.at[chip, core, b], partner) for b in range(NS)]
     own = weight.at[chip, core]
-    own_x = [same(own, peer) for peer in (right, left, across)]
+    own_x = [same(own, peer) for peer in (across, right, left)]
     own_shared = [same(own, sibling)]
 
     loads[2].wait()
@@ -116,7 +116,7 @@
     lax.fori_loop(0, NY, scale_chip, 0)
 
     def own_near():
-        for copy, n in zip(own_x, (-1, 1, 2)):
+        for copy, n in zip(own_x[1:] + own_x[:1], (-1, 1, 2)):
             copy.wait_recv()
             own_shared.append(same(weight.at[hi * NX + xp(n), core], sibling))
 
@@ -138,11 +138,11 @@
     def far_1(b):
         far_z[b].wait_recv()
         w = weight.at[far * NX + x, core, b]
-        far_x[b] = [same(w, peer) for peer in (right, left, across)]
+        far_x[b] = [same(w, peer) for peer in (across, right, left)]
         far_shared[b].append(same(w, sibling))
 
     def far_2(b):
-        for copy, n in zip(far_x[b], (-1, 1, 2)):
+        for copy, n in zip(far_x[b][1:] + far_x[b][:1], (-1, 1, 2)):
             copy.wait_recv()
             far_shared[b].append(same(weight.at[far * NX + xp(n), core, b], sibling))
 

time: 82.3 us -> 80.9 us (0.983)
  no operation moved by 1% of the time
where the time goes in v4:
time: 80.9 us; the launch traced here: 80 us
  Pallas kernels  77.3 us (96%)
  local copies, waits for them, and re-layouts  2.03 us (3%)
    pallas_call x1, Pallas kernels, local(): pl.pallas_call(kernel, name='expert_down', out_shape=(jax.ShapeDtypeStruc...  77.3 us
    unnamed x3, local copies, waits for them, and re-layouts  2.03 us

profile of v4, /device:TPU:6, one launch (start us, length us, event | category | flops | bytes accessed | tf_op | source)
XLA Modules:
  0.0 80.0 jit_solution(9391038842916579650)
XLA Ops:
  0.6 77.3 %expert_down.1 = (bf16[256,128]{1,0:T(8,128)(2,1)S(1)}, bf16[256,256]{1,0:T(8,128)(2,1)S(1)}, f32[256,384]{1,0:T(8,128)S(1)}) custom-call(bf16[256,256]{1,0:T(8,128)(2,1)} %acts_ref.1, bf16[256,384]{1,0:T(8,128)(2,1)} %codes_ref.1, f32[3,256]{1,0:T(4,128)} %scales_ref.1, s32[2,256]{1,0:T(2,128)} %bitcast.2, f32[2,256]{1,0:T(2,128)} %bitcast.3, ...), custom_call_target="tpu_custom_call" | custom-call | flops 2500000000 | bytes 8000000 | tf_op jit(solution)/shard_map/expert_down/pallas_call | solution.py:342
  78.0 0.6 copy.12
  78.6 0.7 copy.13
  79.3 0.7 copy.14
